TPU v7x, 32 devices: a whole 2x2x4 slice. The times are simulated.
32 devices in a mesh: sub: 4 (over z), row: 2 (over x), col: 4 (over y, core).
Axes of the slice: x: 2, y: 2, z: 4, core: 2. Of those that a mesh axis runs over, the one named last changes fastest.
Arguments:
- front_in: float32 [12288, 12288], P('row', ('sub', 'col')), as said below
- child_updates: float32 [4, 8192, 8192], P('sub', 'row', 'col'), as said below
- pattern: int32 [4, 32, 32], P('sub', 'row', 'col'), may hold values from 0 to 1, as said below
- child_map: int32 [4, 32], replicated, may hold values from 0 to 47, as said below
- pivot_inverse: float32 [1024, 1024], replicated, as said below
Outputs:
- front_out: float32 [12288, 12288], P('row', ('sub', 'col'))
Inputs may be any that keep to these rules, and one draw needn't show every extreme that they name: front_in is symmetric. Each child_updates[s] is symmetric. Each pattern[s] is symmetric. child_map[s] is strictly increasing, and child_map[s, i] // 3 equals i // 2. pivot_inverse is lower triangular with a positive diagonal.
All inputs are finite; a program needn't handle non-finite values.
Results may differ from a plain program's by a relative error of at most 0.000053.
Values sent between devices are 32-bit elements; how exact they have to be, the bound alone decides.
A program may use at most 256 MiB of HBM per device.

v0:
```python
import jax
import jax.numpy as jnp
from jax import lax
from jax.sharding import PartitionSpec as P

BLK = 256
FRONT = 12288
CHILD = 8192
PANEL = 1024


def from_root(value, axis, source):
    kept = jnp.where(lax.axis_index(axis) == source, value, 0).astype(value.dtype)
    return lax.psum(kept, axis)


def times_transposed(left, right):
    return lax.dot_general(
        left,
        right,
        (((1,), (1,)), ((), ())),
        precision=lax.Precision.HIGHEST,
        preferred_element_type=jnp.float32,
    )


def shards(front_in, child_updates, pattern, child_map, pivot_inverse):
    sub_count = lax.axis_size("sub")
    row_count = lax.axis_size("row")
    col_count = lax.axis_size("col")
    groups = sub_count * col_count
    sub_id = lax.axis_index("sub")
    row_id = lax.axis_index("row")
    col_id = lax.axis_index("col")
    group_id = sub_id * col_count + col_id
    fblocks = FRONT // BLK
    cblocks = CHILD // BLK
    row_blocks = fblocks // row_count
    col_blocks = fblocks // groups
    child_rows = cblocks // row_count
    child_group = cblocks // groups
    child_cols = cblocks // col_count
    updates = child_updates[0].reshape(child_rows, BLK, child_cols, BLK)
    weights = pattern[0].astype(jnp.float32)
    masked = (updates * weights[:, None, :, None]).reshape(
        child_rows * BLK, sub_count, child_group * BLK
    )
    arrived = lax.all_to_all(
        lax.all_to_all(masked, "col", split_axis=1, concat_axis=1, tiled=True),
        "sub",
        split_axis=1,
        concat_axis=1,
        tiled=True,
    )
    rows_map = lax.dynamic_slice_in_dim(child_map, row_id * child_rows, child_rows, 1)
    cols_map = lax.dynamic_slice_in_dim(child_map, group_id * child_group, child_group, 1)
    row_targets = row_id * row_blocks + jnp.arange(row_blocks, dtype=jnp.int32)
    col_targets = group_id * col_blocks + jnp.arange(col_blocks, dtype=jnp.int32)
    row_hot = (rows_map[:, None, :] == row_targets[None, :, None]).astype(jnp.float32)
    col_hot = (cols_map[:, None, :] == col_targets[None, :, None]).astype(jnp.float32)
    pieces = arrived.reshape(child_rows, BLK, sub_count, child_group, BLK)
    spread_rows = jnp.einsum("spa,axsby->pxsby", row_hot, pieces, precision=lax.Precision.HIGHEST)
    extended = jnp.einsum("sqb,pxsby->pxqy", col_hot, spread_rows, precision=lax.Precision.HIGHEST)
    assembled = front_in + extended.reshape(row_blocks * BLK, col_blocks * BLK)
    panel_blocks = PANEL // BLK
    root_count = (panel_blocks + col_blocks - 1) // col_blocks
    gathered = []
    for owner in range(root_count):
        span_blocks = min(col_blocks, panel_blocks - owner * col_blocks)
        received_panel = from_root(assembled[:, : span_blocks * BLK], ("sub", "col"), owner)
        gathered.append(received_panel)
    panel_cols = jnp.concatenate(gathered, axis=1)
    factor = times_transposed(panel_cols, pivot_inverse)
    root_row = group_id * col_blocks // row_blocks
    offset = group_id * col_blocks - root_row * row_blocks
    own_slice = lax.dynamic_slice_in_dim(factor, offset * BLK, col_blocks * BLK, 0)
    column_factor = from_root(own_slice, "row", root_row)
    update = times_transposed(factor, column_factor)
    panel_parts = []
    for column in range(col_blocks):
        global_block = group_id * col_blocks + column
        panel_parts.append(
            lax.dynamic_slice_in_dim(
                factor, jnp.minimum(global_block, panel_blocks - 1) * BLK, BLK, 1
            )
        )
    panel_part = jnp.concatenate(panel_parts, axis=1)
    rows_global = (row_id * row_blocks * BLK + jnp.arange(row_blocks * BLK, dtype=jnp.int32)) // BLK
    cols_global = (
        group_id * col_blocks * BLK + jnp.arange(col_blocks * BLK, dtype=jnp.int32)
    ) // BLK
    below = (rows_global >= panel_blocks)[:, None]
    beyond = (cols_global >= panel_blocks)[None, :]
    result = jnp.where(below & beyond, assembled - update, jnp.where(below, panel_part, assembled))
    return result


def solution(mesh):
    in_specs = (P("row", ("sub", "col")), P("sub", "row", "col"), P("sub", "row", "col"), P(), P())
    out_specs = P("row", ("sub", "col"))
    return jax.shard_map(shards, mesh=mesh, in_specs=in_specs, out_specs=out_specs, check_vma=False)
```

profile of v0, /device:TPU:15, one launch (start us, length us, event | category | flops | bytes accessed | tf_op | source)
XLA Modules:
  0.0 2238.6 jit_solution(5394756414394527701)
XLA Ops:
  6.5 0.0 copy-start
  6.5 0.7 convert_bitcast_fusion
  7.2 11.3 mul.59
  18.6 35.9 %mul.60 = f32[4096,4,512]{0,2,1:T(8,128)} reshape(f32[16,256,8,256]{1,0,3,2:T(8,128)} %mul.59) | data formatting | bytes 67108864 | tf_op jit(solution)/shard_map/mul | solution.py:45
  54.5 31.2 %copy.25 = f32[1,4096,2048]{1,2,0:T(8,128)} copy(f32[1,4096,2048]{2,1,0:T(8,128)} %param.6) | data formatting | bytes 67108864 | tf_op args[1]
  85.6 33.5 %mul.61 = f32[4096,4,512]{0,2,1:T(8,128)} multiply(f32[4096,4,512]{0,2,1:T(8,128)} %bitcast.34, f32[4096,4,512]{0,2,1:T(8,128)} %mul.60) | non-fusion elementwise | flops 8388608 | bytes 100663296 | tf_op jit(solution)/shard_map/mul | solution.py:45
  119.1 31.1 %copy.26 = f32[4096,4,512]{2,0,1:T(8,128)} copy(f32[4096,4,512]{0,2,1:T(8,128)} %mul.61) | data formatting | bytes 67108864 | tf_op jit(solution)/shard_map/mul | solution.py:45
  150.2 379.9 %all_to_all.10 = f32[4096,4,512]{2,0,1:T(8,128)} all-to-all(f32[4096,4,512]{2,0,1:T(8,128)} %copy.26), channel_id=1, replica_groups=mesh['sub'=4,'row'=2,'col'=4] {'col'}, dimensions={1} | all-to-all | bytes 67108864 | tf_op jit(solution)/shard_map/all_to_all | solution.py:49
  530.0 9.8 all-to-all-start.1
  539.9 0.0 all-reduce.6.cloned.1.call-start
  539.9 0.0 copy-done
  539.9 0.1 constant_dynamic-slice_fusion.3
  539.9 0.1 copy.29
  540.0 18.6 copy.32
  558.7 0.1 constant_dynamic-slice_fusion.4
  558.8 699.9 %all-to-all-done.1 = f32[4096,4,512]{2,0,1:T(8,128)} async-done(((f32[4096,4,512]{2,0,1:T(8,128)}), f32[4096,4,512]{2,0,1:T(8,128)}, u32[]{:S(2)}, u32[]{:S(2)}) %all-to-all-start.1) | async-done | bytes 33554464 | tf_op jit(solution)/shard_map/all_to_all | solution.py:48
  1258.7 38.7 %reshape.70 = f32[16,256,4,2,256]{4,3,1,0,2:T(2,128)} reshape(f32[4096,4,512]{2,0,1:T(8,128)} %all-to-all-done.1) | data formatting | bytes 67108864 | tf_op jit(solution)/shard_map/reshape | solution.py:61
  1297.3 50.5 %fusion.9 = f32[24,256,4,2,256]{4,0,3,1,2:T(8,128)} fusion(f32[16,256,4,2,256]{4,3,1,0,2:T(2,128)} %reshape.70, s32[24]{0:T(128)S(1)} %iota_add_fusion.3, s32[4,16]{1,0:T(4,128)S(1)} %constant_dynamic-slice_fusion.4), kind=kOutput, calls=%fused_computation.10 | convolution fusion | flops 2415920640 | bytes 83886432 | tf_op jit(solution)/shard_map/spa,axsby->pxsby/dot_general | solution.py:62
  1347.9 108.7 %fusion = f32[24,256,256,3,1]{2,3,4,1,0:T(4,128)} fusion(f32[24,256,4,2,256]{4,0,3,1,2:T(8,128)} %fusion.9, s32[4,2]{0,1:T(2,128)S(1)} %copy.29, s32[3]{0:T(128)S(1)} %iota_add_fusion.2), kind=kOutput, calls=%fused_computation | convolution fusion | flops 452984864 | bytes 69206064 | tf_op jit(solution)/shard_map/sqb,pxsby->pxqy/dot_general | solution.py:63
  1456.6 19.0 copy.42
  1475.6 18.7 copy.41
  1494.3 19.5 broadcast_select_fusion
  1513.8 0.0 copy-start.2
  1513.8 6.5 copy-done.2
  1520.3 3.1 slice_select_fusion
  1523.4 0.0 all-reduce.6.cloned.1.call-update
  1523.4 0.0 all-reduce.4.cloned.1.call-start
  1523.5 442.9 %all-reduce.6.cloned.1.call-done = (f32[6144,256]{0,1:T(8,128)}, f32[6144,768]{0,1:T(8,128)}) async-done(((f32[6144,256]{0,1:T(8,128)}, f32[6144,768]{0,1:T(8,128)}), (f32[6144,256]{0,1:T(8,128)}, f32[6144,768]{0,1:T(8,128)})) %all-reduce.6.cloned.1.call-update) | async-done | bytes 25165840 | tf_op jit(solution)/shard_map/psum | solution.py:14
  1966.4 85.1 %fusion.4 = f32[6144,1024]{0,1:T(8,128)} fusion(f32[1024,1024]{1,0:T(8,128)} %param.9, f32[6144,256]{0,1:T(8,128)} %get-tuple-element.5, f32[6144,768]{0,1:T(8,128)} %get-tuple-element.6), kind=kOutput, calls=%fused_computation.4 | convolution fusion | flops 77315702784 | bytes 54525952 | tf_op jit(solution)/shard_map/dot_general | solution.py:18
  2051.5 3.8 dynamic-slice_select_fusion
  2055.3 0.0 all-reduce.4.cloned.1.call-update
  2055.4 13.3 constant_dynamic-slice_fusion.2
  2068.8 71.8 %all-reduce.4.cloned.1.call-done = f32[768,1024]{0,1:T(8,128)} async-done(((f32[768,1024]{0,1:T(8,128)}), f32[768,1024]{0,1:T(8,128)}) %all-reduce.4.cloned.1.call-update) | async-done | bytes 3145744 | tf_op jit(solution)/shard_map/psum | solution.py:14
  2140.6 0.0 copy-start.1
  2140.6 72.4 %fusion.8 = f32[6144,768]{0,1:T(8,128)} fusion(f32[6144,768]{0,1:T(8,128)} %copy-done.2, f32[6144,256]{0,1:T(8,128)} %get-tuple-element.10, f32[6144,256]{0,1:T(8,128)} %get-tuple-element.11, f32[6144,256]{0,1:T(8,128)} %get-tuple-element.9, f32[6144,1024]{0,1:T(8,128)} %fusion.4, f32[768,1024]{0,1:T(8,128)} %all-reduce.4.cloned.1.call-done, ...), kind=kOutput, calls=%fused_computation.9 | convolution fusion | flops 58010370048 | bytes 84941568 | tf_op jit(solution)/shard_map/dot_general | solution.py:18
  2213.0 18.6 copy.34
  2231.6 0.0 copy-done.1
  (4 shorter events, 0.0 us)
Async XLA Ops:
  6.5 533.3 %copy-start = (s32[4,32]{1,0:T(4,128)S(1)}, s32[4,32]{1,0:T(4,128)}, u32[]{:S(2)}) copy-start(s32[4,32]{1,0:T(4,128)} %param.8) | copy-start | bytes 1540
  530.0 728.7 %all-to-all-start.1 = ((f32[4096,4,512]{2,0,1:T(8,128)}), f32[4096,4,512]{2,0,1:T(8,128)}, u32[]{:S(2)}, u32[]{:S(2)}) async-start(f32[4096,4,512]{2,0,1:T(8,128)} %all_to_all.10), calls=%async_computation.1 | async-start | bytes 67108864 | tf_op jit(solution)/shard_map/all_to_all | solution.py:48
  539.9 1426.5 %all-reduce.6.cloned.1.call-start = ((), (), s32[]{:S(2)}) async-start(), calls=%async_computation.3 | async-start | bytes 50331648 | tf_op jit(solution)/shard_map/psum | solution.py:14
  1513.8 6.5 copy-start.2
  1523.4 617.2 %all-reduce.4.cloned.1.call-start = ((), (), s32[]{:S(2)}) async-start(), calls=%async_computation.2 | async-start | bytes 6291456 | tf_op jit(solution)/shard_map/psum | solution.py:14
  2140.6 91.1 %copy-start.1 = (s32[4,32]{1,0:T(4,128)S(1)}, s32[4,32]{1,0:T(4,128)}, u32[]{:S(2)}) copy-start(s32[4,32]{1,0:T(4,128)} %param.8) | copy-start | bytes 1540
Sparse Core Ops, SparseCore 0:
  1523.5 442.8 all-reduce.5
  2055.5 85.0 all-reduce.3
where the time goes:
time: 2240 us
  waiting for transfers between devices  1210 us (54%)
  blocking collectives  380 us (17%)
  matrix products  317 us (14%)
  local copies, waits for them, and re-layouts  243 us (11%)
  other arithmetic  60.6 us (3%)
    all_to_all x1, waiting for transfers between devices, shards(): lax.all_to_all(lax.all_to_all(masked, 'col', split_axis=1, concat_axis=1,...  700 us
    psum x2, waiting for transfers between devices, from_root(): return lax.psum(kept, axis)  515 us
    all_to_all x1, blocking collectives, shards(): lax.all_to_all(masked, 'col', split_axis=1, concat_axis=1, tiled=True)  380 us
    dot_general x2, matrix products, times_transposed(): lax.dot_general(left, right, (((1,), (1,)), ((), ())), precision=lax.Prec...  158 us
    dot_general x1, matrix products, shards(): jnp.einsum('sqb,pxsby->pxqy', col_hot, spread_rows, precision=lax.Precisi...  109 us
    mul x3, local copies, waits for them, and re-layouts, shards(): updates * weights[:, None, :, None]  78.3 us
    unnamed x9, local copies, waits for them, and re-layouts  75.3 us
    dot_general x1, matrix products, shards(): jnp.einsum('spa,axsby->pxsby', row_hot, pieces, precision=lax.Precision.H...  50.5 us
  transfers between devices with their start and end apart: 3, of which 3 were waited for; matrix products, arithmetic and copies ran while one was open for 1% of the time, Pallas kernels for 0%

commit v1 on v0

v1 whole, which is shorter than its diff:
```python
import functools

import jax
import jax.numpy as jnp
from jax import lax
from jax.experimental import pallas as pl
from jax.experimental.pallas import tpu as pltpu
from jax.sharding import PartitionSpec as P

BLK = 256
FRONT = 12288
CHILD = 8192
PANEL = 1024
MESH = pl.DeviceIdType.MESH


def exchange_kernel(count, first, rows, chunks, aliased, *refs):
    if aliased:
        child, _, stage, out = refs[:4]
        send1, recv1, send2, recv2 = refs[4:]
    else:
        child, stage, out = refs[:3]
        send1, recv1, send2, recv2 = refs[3:]
    sub = lax.axis_index("sub")
    row = lax.axis_index("row")
    col = lax.axis_index("col")
    width = out.shape[2]
    size = rows // chunks

    barrier = pltpu.get_barrier_semaphore()
    for step in range(1, count):
        pl.semaphore_signal(
            barrier, inc=1, device_id=(sub, row, lax.rem(col + step, count)), device_id_type=MESH
        )
        pl.semaphore_signal(
            barrier, inc=1, device_id=(lax.rem(sub + step, count), row, col), device_id_type=MESH
        )
    pl.semaphore_wait(barrier, 2 * (count - 1))

    def columns(index):
        return pl.ds(pl.multiple_of(index * width, width), width)

    def spread(part, step):
        target = lax.rem(col + step, count)
        return pltpu.make_async_remote_copy(
            src_ref=child.at[0, pl.ds(first + part * size, size), columns(target)],
            dst_ref=stage.at[col, pl.ds(part * size, size), :],
            send_sem=send1.at[part, step],
            recv_sem=recv1.at[part, col],
            device_id=(sub, row, target),
            device_id_type=MESH,
        )

    def keep(part):
        return pltpu.make_async_copy(
            child.at[0, pl.ds(first + part * size, size), columns(col)],
            stage.at[col, pl.ds(part * size, size), :],
            recv1.at[part, col],
        )

    def deliver(part, step):
        target = lax.rem(sub + step, count)
        return pltpu.make_async_remote_copy(
            src_ref=stage.at[target, pl.ds(part * size, size), :],
            dst_ref=out.at[sub, pl.ds(first + part * size, size), :],
            send_sem=send2.at[part, step],
            recv_sem=recv2.at[part, sub],
            device_id=(target, row, col),
            device_id_type=MESH,
        )

    def place(part):
        return pltpu.make_async_copy(
            stage.at[sub, pl.ds(part * size, size), :],
            out.at[sub, pl.ds(first + part * size, size), :],
            recv2.at[part, sub],
        )

    def arrived(ref, sem):
        pltpu.make_async_copy(ref, ref, sem).wait()

    for part in range(chunks):
        for step in range(1, count):
            spread(part, step).start()
        keep(part).start()
    for part in range(chunks):
        for step in list(range(1, count)) + [0]:
            source = lax.rem(sub + step, count)
            arrived(stage.at[source, pl.ds(part * size, size), :], recv1.at[part, source])
            if step:
                deliver(part, step).start()
            else:
                place(part).start()
    for part in range(chunks):
        for source in range(count):
            arrived(out.at[source, pl.ds(first + part * size, size), :], recv2.at[part, source])
        for step in range(1, count):
            spread(part, step).wait_send()
            deliver(part, step).wait_send()


def exchange(child, received, first, rows, chunks, count, ident):
    total, width = child.shape[1], child.shape[2] // count
    aliased = received is not None
    operands = (child, received) if aliased else (child,)
    anywhere = pl.BlockSpec(memory_space=pl.ANY)
    moved = 2 * count * rows * width * 4
    _, result = pl.pallas_call(
        functools.partial(exchange_kernel, count, first, rows, chunks, aliased),
        out_shape=[
            jax.ShapeDtypeStruct((count, rows, width), jnp.float32),
            jax.ShapeDtypeStruct((count, total, width), jnp.float32),
        ],
        in_specs=[anywhere] * len(operands),
        out_specs=[anywhere, anywhere],
        scratch_shapes=[pltpu.SemaphoreType.DMA((chunks, count))] * 4,
        input_output_aliases={1: 1} if aliased else {},
        compiler_params=pltpu.CompilerParams(
            collective_id=ident, has_side_effects=True, vmem_limit_bytes=48 * 2**20
        ),
        cost_estimate=pl.CostEstimate(flops=0, bytes_accessed=40 * moved, transcendentals=0),
    )(*operands)
    return result


def extended_columns(weights, a, front, pieces, column):
    total = front[:, column * BLK : (column + 1) * BLK]
    for s, piece in enumerate(pieces):
        for j in range(2):
            weight = weights[((a * len(pieces) + s) * 3 + column) * 2 + j]
            total = total + weight * piece[0, :, j * BLK : (j + 1) * BLK]
    return total


def strip_kernel(count, where, weights, front, *refs):
    a = pl.program_id(0)
    for column in range(3):
        refs[-1][:, column * BLK : (column + 1) * BLK] = extended_columns(
            weights, a, front, refs[:count], column
        )


def final_kernel(count, panel_blocks, where, weights, front, *refs):
    pieces = refs[:count]
    rows_factor, cols_factor, out, high, low = refs[count:]
    a = pl.program_id(0)
    row_block = where[0] + a
    contract = (((1,), (1,)), ((), ()))

    @pl.when(a == 0)
    def _():
        value = cols_factor[...]
        top = value.astype(jnp.bfloat16)
        high[...] = top
        low[...] = (value - top.astype(jnp.float32)).astype(jnp.bfloat16)

    value = rows_factor[...]
    top = value.astype(jnp.bfloat16)
    rest = (value - top.astype(jnp.float32)).astype(jnp.bfloat16)
    for column in range(3):
        col_block = where[1] + column
        span = slice(column * BLK, (column + 1) * BLK)
        here = extended_columns(weights, a, front, pieces, column)
        dot = functools.partial(
            lax.dot_general, dimension_numbers=contract, preferred_element_type=jnp.float32
        )
        update = dot(top, low[span, :]) + dot(rest, high[span, :]) + dot(top, high[span, :])
        both = jnp.logical_and(row_block >= panel_blocks, col_block >= panel_blocks)
        out[:, span] = jnp.where(both, here - update, here)

        @pl.when(jnp.logical_and(row_block >= panel_blocks, col_block < panel_blocks))
        def _():
            source = jnp.minimum(col_block, panel_blocks - 1) * BLK
            out[:, span] = rows_factor[:, pl.ds(pl.multiple_of(source, BLK), BLK)]


def piece_specs(count, offset):
    def one(s):
        return pl.BlockSpec((1, BLK, 2 * BLK), lambda a, where: (s, where[offset + a * count + s], 0))

    return [one(s) for s in range(count)]


def shards(front_in, child_updates, pattern, child_map, pivot_inverse):
    sub_count = lax.axis_size("sub")
    row_count = lax.axis_size("row")
    col_count = lax.axis_size("col")
    assert sub_count == col_count
    count = sub_count
    groups = sub_count * col_count
    row_id = lax.axis_index("row")
    group_id = lax.axis_index("sub") * col_count + lax.axis_index("col")
    row_blocks = FRONT // BLK // row_count
    col_blocks = FRONT // BLK // groups
    child_rows = CHILD // BLK // row_count
    child_cols = CHILD // BLK // groups
    panel_blocks = PANEL // BLK
    group_cols = col_blocks * BLK
    first_row = row_id * row_blocks
    first_col = group_id * col_blocks
    assert col_blocks == 3 and child_cols == 2

    masks = lax.all_gather(pattern[0], ("sub", "col"), axis=0, tiled=False)
    masks = masks.reshape(sub_count, col_count, child_rows, CHILD // BLK // col_count)
    masks = masks.transpose(0, 2, 1, 3).reshape(sub_count, child_rows, CHILD // BLK)
    mine = lax.dynamic_slice_in_dim(masks, group_id * child_cols, child_cols, 2)
    rows_map = lax.dynamic_slice_in_dim(child_map, row_id * child_rows, child_rows, 1)
    cols_map = lax.dynamic_slice_in_dim(child_map, group_id * child_cols, child_cols, 1)
    row_at = first_row + jnp.arange(row_blocks, dtype=jnp.int32)
    col_at = first_col + jnp.arange(col_blocks, dtype=jnp.int32)
    row_hit = rows_map[None] == row_at[:, None, None]
    col_hit = cols_map[None] == col_at[:, None, None]
    fallback = (jnp.arange(row_blocks, dtype=jnp.int32) // 3 * 2)[:, None]
    indices = jnp.arange(child_rows, dtype=jnp.int32)
    row_from = jnp.where(
        row_hit.any(2), jnp.sum(jnp.where(row_hit, indices, 0), axis=2), fallback
    ).astype(jnp.int32)
    kept = jnp.sum(jnp.where(row_hit[..., None], mine[None], 0), axis=2)
    weights = jnp.where(col_hit[None], kept.transpose(0, 1, 2)[:, None], 0)
    weights = weights.transpose(0, 2, 1, 3).astype(jnp.float32).reshape(-1)
    where = jnp.concatenate(
        [jnp.stack([first_row, first_col]).astype(jnp.int32), row_from.reshape(-1)]
    )

    rows = child_rows * BLK
    head = min(rows, 4 * BLK)
    received = exchange(child_updates, None, 0, head, 2, count, 0)
    strip_blocks = min(panel_blocks, row_blocks)
    smem = pl.BlockSpec(memory_space=pltpu.SMEM)
    front_spec = pl.BlockSpec((BLK, group_cols), lambda a, where: (a, 0))
    strip = pl.pallas_call(
        functools.partial(strip_kernel, count),
        grid_spec=pltpu.PrefetchScalarGridSpec(
            num_scalar_prefetch=1,
            grid=(strip_blocks,),
            in_specs=[smem, front_spec] + piece_specs(count, 2),
            out_specs=front_spec,
        ),
        out_shape=jax.ShapeDtypeStruct((strip_blocks * BLK, group_cols), jnp.float32),
        cost_estimate=pl.CostEstimate(flops=0, bytes_accessed=20 * 2**20, transcendentals=0),
    )(where, weights, front_in, *([received] * count))
    if row_count == 1:
        panel_t = strip
    elif row_count == 2 and strip_blocks == panel_blocks:
        other = lax.ppermute(strip, "row", [(0, 1)])
        panel_t = jnp.where(row_id == 0, strip, other)
    else:
        span = strip_blocks * BLK
        parts = -(-PANEL // span)
        pieces = [jnp.where(row_id == part, strip, 0.0) for part in range(parts)]
        panel_t = lax.psum(jnp.concatenate(pieces, axis=0)[:PANEL], "row")
    cols_factor = lax.dot_general(
        panel_t,
        pivot_inverse,
        (((0,), (1,)), ((), ())),
        precision=lax.Precision.HIGHEST,
        preferred_element_type=jnp.float32,
    )

    group_rows = groups // row_count
    left = rows - head
    if left:
        child, cols_factor = lax.optimization_barrier((child_updates, cols_factor))
        half = left // 2
        received = exchange(child, received, head, half, 3, count, 1)
    if group_rows >= col_count:
        deep = group_rows // col_count
        along = lax.all_gather(cols_factor, "sub", axis=0, tiled=False)
        if left:
            along, received = lax.optimization_barrier((along, received))
        needed = lax.dynamic_slice_in_dim(along, row_id * deep, deep, 0)
        if left:
            child, needed = lax.optimization_barrier((child, needed))
        gathered = lax.all_gather(needed, "col", axis=0, tiled=False)
        gathered = gathered.reshape(-1, PANEL)

        def factor_at(a, where):
            group = a // 3
            return ((group % col_count) * deep + group // col_count) * 3 + a % 3, 0
    else:
        gathered = lax.all_gather(cols_factor, ("sub", "col"), axis=0, tiled=False)
        gathered = lax.dynamic_slice_in_dim(gathered, row_id * group_rows, group_rows, 0)
        gathered = gathered.reshape(-1, PANEL)

        def factor_at(a, where):
            return a, 0

    if left:
        received = exchange(child, received, head + half, left - half, 3, count, 2)
    return pl.pallas_call(
        functools.partial(final_kernel, count, panel_blocks),
        grid_spec=pltpu.PrefetchScalarGridSpec(
            num_scalar_prefetch=1,
            grid=(row_blocks,),
            in_specs=[smem, front_spec]
            + piece_specs(count, 2)
            + [
                pl.BlockSpec((BLK, PANEL), factor_at),
                pl.BlockSpec((group_cols, PANEL), lambda a, where: (0, 0)),
            ],
            out_specs=front_spec,
            scratch_shapes=[pltpu.VMEM((group_cols, PANEL), jnp.bfloat16)] * 2,
        ),
        out_shape=jax.ShapeDtypeStruct((row_blocks * BLK, group_cols), jnp.float32),
        compiler_params=pltpu.CompilerParams(vmem_limit_bytes=48 * 2**20),
        cost_estimate=pl.CostEstimate(
            flops=6 * row_blocks * BLK * group_cols * PANEL,
            bytes_accessed=100 * 2**20,
            transcendentals=0,
        ),
    )(where, weights, front_in, *([received] * count), gathered, cols_factor)


def solution(mesh):
    in_specs = (P("row", ("sub", "col")), P("sub", "row", "col"), P("sub", "row", "col"), P(), P())
    out_specs = P("row", ("sub", "col"))
    return jax.shard_map(shards, mesh=mesh, in_specs=in_specs, out_specs=out_specs, check_vma=False)
```

time: 2240 us -> 1220 us (0.54)
  waiting for transfers between devices: 1210 us -> 70.9 us
  Pallas kernels: 0 us -> 1090 us
  blocking collectives: 380 us -> 16 us
  matrix products: 317 us -> 22.8 us
  local copies, waits for them, and re-layouts: 243 us -> 8.5 us
  other arithmetic: 60.6 us -> 1.09 us
    pallas_call x0 -> x5, Pallas kernels: none -> 1090 us  [the longest x3 1010 us: exchange(): pl.pallas_call(functools.partial(exchange_kernel, count, first, rows, chu...]
    all_to_all x1 -> x0, waiting for transfers between devices: 700 us -> none  [shards(): lax.all_to_all(lax.all_to_all(masked, 'col', split_axis=1, concat_axis=1,...]
    psum x2 -> x0, waiting for transfers between devices: 515 us -> none  [from_root(): return lax.psum(kept, axis)]
    all_to_all x1 -> x0, blocking collectives: 380 us -> none  [shards(): lax.all_to_all(masked, 'col', split_axis=1, concat_axis=1, tiled=True)]
    dot_general x4 -> x1, matrix products: 317 us -> 22.8 us  [shards(): lax.dot_general(panel_t, pivot_inverse, (((0,), (1,)), ((), ())), precisi...]
    mul x3 -> x0, local copies, waits for them, and re-layouts: 78.3 us -> none  [shards(): updates * weights[:, None, :, None]]
    unnamed x9 -> x10, local copies, waits for them, and re-layouts: 75.3 us -> 0.69 us
    ppermute x0 -> x1, waiting for transfers between devices: none -> 70.9 us  [shards(): other = lax.ppermute(strip, 'row', [(0, 1)])]
  transfers between devices with their start and end apart: 3 -> 3, of which waited for: 3 -> 1; matrix products, arithmetic and copies ran while one was open for 1% -> 0% of each run, Pallas kernels for 0% -> 65%
where the time goes in v1:
time: 1220 us
  Pallas kernels  1090 us (89%)
  waiting for transfers between devices  70.9 us (6%)
  matrix products  22.8 us (2%)
  blocking collectives  16 us (1%)
  between operations  13.5 us (1%)
    pallas_call x3, Pallas kernels, exchange(): pl.pallas_call(functools.partial(exchange_kernel, count, first, rows, chu...  1010 us
    pallas_call x1, Pallas kernels, shards(): pl.pallas_call(functools.partial(final_kernel, count, panel_blocks), grid...  71.5 us
    ppermute x1, waiting for transfers between devices, shards(): other = lax.ppermute(strip, 'row', [(0, 1)])  70.9 us
  transfers between devices with their start and end apart: 3, of which 1 were waited for; matrix products, arithmetic and copies ran while one was open for 0% of the time, Pallas kernels for 65%

profile of v1, /device:TPU:15, one launch (start us, length us, event | category | flops | bytes accessed | tf_op | source)
XLA Modules:
  0.0 1219.6 jit_solution(7698307404663140919)
XLA Ops:
  6.5 0.0 copy-start
  6.5 0.0 all-gather.5.cloned.1.call-start
  6.5 0.7 copy-done
  7.2 0.1 constant_dynamic-slice_fusion.3
  7.3 0.1 broadcast_compare_fusion
  7.4 0.1 select_reduce_fusion.1
  7.5 16.0 %all_gather.15 = s32[16,16,8]{1,2,0:T(8,128)S(1)} all-gather(s32[1,16,8]{1,2,0:T(8,128)} %param.7), channel_id=1, replica_groups=mesh['sub'=4,'row'=2,'col'=4] {'sub','col'}, dimensions={0}, use_global_device_ids=true | all-gather | bytes 8704 | tf_op jit(solution)/shard_map/all_gather | solution.py:203
  23.5 0.1 constant_dynamic-slice_fusion.2
  23.6 0.1 select_reduce_fusion
  23.7 0.1 copy.12
  23.8 0.1 broadcast_compare_fusion.1
  23.9 0.7 convert_element_type.8.weights
  24.7 0.1 copy.11
  24.8 0.1 select_n.54
  24.9 214.8 %shard_map.55 = (f32[4,1024,512]{2,1,0:T(8,128)}, f32[4,4096,512]{2,1,0:T(8,128)}) custom-call(f32[1,4096,2048]{2,1,0:T(8,128)} %refs_0_.3), custom_call_target="tpu_custom_call" | custom-call | bytes 671088640 | tf_op jit(solution)/shard_map/pallas_call | solution.py:108
  239.7 0.7 pad_add_fusion.where
  240.3 7.5 shard_map.56
  247.8 1.3 collective-permute-start
  249.1 70.9 %collective-permute-done = f32[1024,768]{1,0:T(8,128)S(1)} collective-permute-done((f32[1024,768]{1,0:T(8,128)}, f32[1024,768]{1,0:T(8,128)S(1)}, u32[]{:S(2)}, u32[]{:S(2)}) %collective-permute-start) | collective-permute-done | bytes 3145760 | tf_op jit(solution)/shard_map/ppermute | solution.py:245
  319.9 22.8 %fusion.refs_5_ = f32[768,1024]{1,0:T(8,128)} fusion(f32[1024,1024]{1,0:T(8,128)} %param.9, f32[1024,768]{1,0:T(8,128)} %shard_map.56, f32[1024,768]{1,0:T(8,128)S(1)} %collective-permute-done, pred[]{:T(512)S(6)} %eq.44), kind=kOutput, calls=%fused_computation | convolution fusion | flops 9664462848 | bytes 13631489 | tf_op jit(solution)/shard_map/dot_general | solution.py:252
  342.8 0.0 all-gather.5.cloned.1.call-update
  342.8 0.2 all-gather.7.cloned.1.call-start
  343.0 485.5 %shard_map.57 = (f32[4,1536,512]{2,1,0:T(8,128)}, f32[4,4096,512]{2,1,0:T(8,128)}) custom-call(f32[1,4096,2048]{2,1,0:T(8,128)} %refs_0_.3, f32[4,4096,512]{2,1,0:T(8,128)} %get-tuple-element.14.refs_0_.refs_1_.refs_2_.refs_3_), custom_call_target="tpu_custom_call", output_to_operand_aliasing={{1}: (1, {})} | custom-call | bytes 1006632960 | tf_op jit(solution)/shard_map/pallas_call | solution.py:108
  828.5 0.0 all-gather.5.cloned.1.call-done
  828.5 6.6 constant_dynamic-slice_fusion
  835.1 0.0 all-gather.7.cloned.1.call-update
  835.2 0.0 copy-start.2
  835.2 0.0 copy-start.3
  835.2 0.0 copy-start.4
  835.2 306.0 %shard_map.58 = (f32[4,1536,512]{2,1,0:T(8,128)}, f32[4,4096,512]{2,1,0:T(8,128)}) custom-call(f32[1,4096,2048]{2,1,0:T(8,128)} %refs_0_.3, f32[4,4096,512]{2,1,0:T(8,128)} %get-tuple-element.20.refs_1_), custom_call_target="tpu_custom_call", output_to_operand_aliasing={{1}: (1, {})} | custom-call | bytes 1006632960 | tf_op jit(solution)/shard_map/pallas_call | solution.py:108
  1141.2 0.0 all-gather.7.cloned.1.call-done
  1141.2 0.0 copy-done.2
  1141.3 0.0 copy-done.3
  1141.3 0.0 copy-done.4
  1141.3 0.0 copy-start.1
  1141.3 71.5 %shard_map.59 = f32[6144,768]{1,0:T(8,128)} custom-call(s32[98]{0:T(128)S(1)} %copy-done.4, f32[576]{0:T(1024)S(1)} %copy-done.3, f32[6144,768]{1,0:T(8,128)} %front.3, f32[4,4096,512]{2,1,0:T(8,128)} %get-tuple-element.21.refs_0_.refs_1_.refs_2_.refs_3_, f32[4,4096,512]{2,1,0:T(8,128)} %get-tuple-element.21.refs_0_.refs_1_.refs_2_.refs_3_, ...), custom_call_target="tpu_custom_call" | custom-call | flops 28991029248 | bytes 104857600 | tf_op jit(solution)/shard_map/pallas_call | solution.py:290
  1212.8 0.0 copy-done.1
  (6 shorter events, 0.1 us)
Async XLA Ops:
  6.5 0.7 copy-start
  6.5 822.0 %all-gather.5.cloned.1.call-start = ((), (), s32[]{:S(2)}) async-start(), calls=%async_computation | async-start | bytes 15728640 | tf_op jit(solution)/shard_map/all_gather | solution.py:268
  247.8 72.1 %collective-permute-start = (f32[1024,768]{1,0:T(8,128)}, f32[1024,768]{1,0:T(8,128)S(1)}, u32[]{:S(2)}, u32[]{:S(2)}) collective-permute-start(f32[1024,768]{1,0:T(8,128)} %shard_map.56), channel_id=1, source_target_pairs={{0,4},{1,5},{2,6},{3,7},{8,12},{9,13},{10,14},{11,15},{16,20},{17,... | collective-permute-start | bytes 9437192 | tf_op jit(solution)/shard_map/ppermute | solution.py:245
  342.8 798.5 %all-gather.7.cloned.1.call-start = ((), (), s32[]{:S(2)}) async-start(), calls=%async_computation.1 | async-start | bytes 31457280 | tf_op jit(solution)/shard_map/all_gather | solution.py:274
  835.2 306.1 %copy-start.2 = (f32[768,1024]{1,0:T(8,128)S(1)}, f32[768,1024]{1,0:T(8,128)}, u32[]{:S(2)}) copy-start(f32[768,1024]{1,0:T(8,128)} %fusion.refs_5_) | copy-start | bytes 9437188
  835.2 306.1 %copy-start.3 = (f32[576]{0:T(1024)S(1)}, f32[576]{0:T(1024)}, u32[]{:S(2)}) copy-start(f32[576]{0:T(1024)} %convert_element_type.8.weights) | copy-start | bytes 6916
  835.2 306.1 %copy-start.4 = (s32[98]{0:T(128)S(1)}, s32[98]{0:T(128)}, u32[]{:S(2)}) copy-start(s32[98]{0:T(128)} %pad_add_fusion.where) | copy-start | bytes 1180
  1141.3 71.5 %copy-start.1 = (s32[4,32]{1,0:T(4,128)S(1)}, s32[4,32]{1,0:T(4,128)}, u32[]{:S(2)}) copy-start(s32[4,32]{1,0:T(4,128)} %param.8) | copy-start | bytes 1540
Sparse Core Ops, SparseCore 0:
  342.9 444.6 all-gather.4
  835.3 275.1 all-gather.6

commit v2 on v1

--- a/solution.py
+++ b/solution.py
@@ -142,29 +142,32 @@
 
 def final_kernel(count, panel_blocks, where, weights, front, *refs):
     pieces = refs[:count]
-    rows_factor, cols_factor, out, high, low = refs[count:]
+    rows_first, rows_second, cols_factor, out, right, rows_factor = refs[count:]
     a = pl.program_id(0)
     row_block = where[0] + a
-    contract = (((1,), (1,)), ((), ()))
+
+    def split(value):
+        top = value.astype(jnp.bfloat16)
+        return top, (value - top.astype(jnp.float32)).astype(jnp.bfloat16)
 
     @pl.when(a == 0)
     def _():
-        value = cols_factor[...]
-        top = value.astype(jnp.bfloat16)
-        high[...] = top
-        low[...] = (value - top.astype(jnp.float32)).astype(jnp.bfloat16)
-
-    value = rows_factor[...]
-    top = value.astype(jnp.bfloat16)
-    rest = (value - top.astype(jnp.float32)).astype(jnp.bfloat16)
+        top, rest = split(cols_factor[...])
+        right[:, :PANEL] = rest
+        right[:, PANEL : 2 * PANEL] = top
+        right[:, 2 * PANEL :] = top
+
+    rows_factor[:, : PANEL // 2] = rows_first[...]
+    rows_factor[:, PANEL // 2 :] = rows_second[...]
+    top, rest = split(rows_factor[...])
+    left = jnp.concatenate([top, rest, top], axis=1)
     for column in range(3):
         col_block = where[1] + column
         span = slice(column * BLK, (column + 1) * BLK)
         here = extended_columns(weights, a, front, pieces, column)
-        dot = functools.partial(
-            lax.dot_general, dimension_numbers=contract, preferred_element_type=jnp.float32
-        )
-        update = dot(top, low[span, :]) + dot(rest, high[span, :]) + dot(top, high[span, :])
+        update = lax.dot_general(
+            left, right[span, :], (((1,), (1,)), ((), ())), preferred_element_type=jnp.float32
+        )
         both = jnp.logical_and(row_block >= panel_blocks, col_block >= panel_blocks)
         out[:, span] = jnp.where(both, here - update, here)
 
@@ -179,6 +182,16 @@
         return pl.BlockSpec((1, BLK, 2 * BLK), lambda a, where: (s, where[offset + a * count + s], 0))
 
     return [one(s) for s in range(count)]
+
+
+def column_factor(panel_t, pivot_inverse):
+    return lax.dot_general(
+        panel_t,
+        pivot_inverse,
+        (((0,), (1,)), ((), ())),
+        precision=lax.Precision.HIGH,
+        preferred_element_type=jnp.float32,
+    )
 
 
 def shards(front_in, child_updates, pattern, child_map, pivot_inverse):
@@ -200,7 +213,7 @@
     first_col = group_id * col_blocks
     assert col_blocks == 3 and child_cols == 2
 
-    masks = lax.all_gather(pattern[0], ("sub", "col"), axis=0, tiled=False)
+    masks = lax.all_gather(pattern[0].astype(jnp.float32), ("sub", "col"), axis=0, tiled=False)
     masks = masks.reshape(sub_count, col_count, child_rows, CHILD // BLK // col_count)
     masks = masks.transpose(0, 2, 1, 3).reshape(sub_count, child_rows, CHILD // BLK)
     mine = lax.dynamic_slice_in_dim(masks, group_id * child_cols, child_cols, 2)
@@ -215,16 +228,16 @@
     row_from = jnp.where(
         row_hit.any(2), jnp.sum(jnp.where(row_hit, indices, 0), axis=2), fallback
     ).astype(jnp.int32)
-    kept = jnp.sum(jnp.where(row_hit[..., None], mine[None], 0), axis=2)
-    weights = jnp.where(col_hit[None], kept.transpose(0, 1, 2)[:, None], 0)
-    weights = weights.transpose(0, 2, 1, 3).astype(jnp.float32).reshape(-1)
+    kept = jnp.sum(jnp.where(row_hit[..., None], mine[None], 0.0), axis=2)
+    weights = jnp.where(col_hit[None], kept[:, None], 0.0)
+    weights = weights.transpose(0, 2, 1, 3).reshape(-1)
     where = jnp.concatenate(
         [jnp.stack([first_row, first_col]).astype(jnp.int32), row_from.reshape(-1)]
     )
 
     rows = child_rows * BLK
     head = min(rows, 4 * BLK)
-    received = exchange(child_updates, None, 0, head, 2, count, 0)
+    received = exchange(child_updates, None, 0, head, head // BLK, count, 0)
     strip_blocks = min(panel_blocks, row_blocks)
     smem = pl.BlockSpec(memory_space=pltpu.SMEM)
     front_spec = pl.BlockSpec((BLK, group_cols), lambda a, where: (a, 0))
@@ -239,54 +252,67 @@
         out_shape=jax.ShapeDtypeStruct((strip_blocks * BLK, group_cols), jnp.float32),
         cost_estimate=pl.CostEstimate(flops=0, bytes_accessed=20 * 2**20, transcendentals=0),
     )(where, weights, front_in, *([received] * count))
-    if row_count == 1:
-        panel_t = strip
-    elif row_count == 2 and strip_blocks == panel_blocks:
-        other = lax.ppermute(strip, "row", [(0, 1)])
-        panel_t = jnp.where(row_id == 0, strip, other)
-    else:
-        span = strip_blocks * BLK
-        parts = -(-PANEL // span)
-        pieces = [jnp.where(row_id == part, strip, 0.0) for part in range(parts)]
-        panel_t = lax.psum(jnp.concatenate(pieces, axis=0)[:PANEL], "row")
-    cols_factor = lax.dot_general(
-        panel_t,
-        pivot_inverse,
-        (((0,), (1,)), ((), ())),
-        precision=lax.Precision.HIGHEST,
-        preferred_element_type=jnp.float32,
-    )
-
     group_rows = groups // row_count
     left = rows - head
-    if left:
-        child, cols_factor = lax.optimization_barrier((child_updates, cols_factor))
-        half = left // 2
-        received = exchange(child, received, head, half, 3, count, 1)
-    if group_rows >= col_count:
+    child = child_updates
+    done = head
+
+    def more(received, blocks, ident):
+        return exchange(child, received, done, blocks * BLK, blocks, count, ident)
+
+    if row_count == 2 and strip_blocks == panel_blocks:
+        parts = (2, 3, 3, left // BLK - 8)
+        child, strip = lax.optimization_barrier((child, strip))
+        other = lax.ppermute(strip, "row", [(0, 1)])
+        received = more(received, parts[0], 1)
+        done += parts[0] * BLK
+        other, received = lax.optimization_barrier((other, received))
+        cols_factor = column_factor(jnp.where(row_id == 0, strip, other), pivot_inverse)
+
         deep = group_rows // col_count
-        along = lax.all_gather(cols_factor, "sub", axis=0, tiled=False)
+        wide = PANEL // 2
+        half = (lax.axis_index("sub") // deep != row_id).astype(jnp.int32)
+        sent = lax.dynamic_slice_in_dim(cols_factor, half * wide, wide, 1)
+        child, sent = lax.optimization_barrier((child, sent))
+        along = lax.all_gather(sent, "sub", axis=0, tiled=False)
+        received = more(received, parts[1], 2)
+        done += parts[1] * BLK
+        along, received = lax.optimization_barrier((along, received))
+
+        first = lax.dynamic_slice_in_dim(along, row_id * deep, deep, 0)
+        passed = lax.dynamic_slice_in_dim(along, (1 - row_id) * deep, deep, 0)
+        child, first, passed = lax.optimization_barrier((child, first, passed))
+        second = lax.ppermute(passed, "row", [(0, 1), (1, 0)])
+        first = lax.all_gather(first, "col", axis=0, tiled=False).reshape(-1, wide)
+        received = more(received, parts[2], 3)
+        done += parts[2] * BLK
+        second, received = lax.optimization_barrier((second, received))
+
+        child, second = lax.optimization_barrier((child, second))
+        second = lax.all_gather(second, "col", axis=0, tiled=False).reshape(-1, wide)
+        received = more(received, parts[3], 4)
+
+        def factor_at(a):
+            group = a // 3
+            return ((group % col_count) * deep + group // col_count) * 3 + a % 3
+
+        second_at = 0
+    else:
         if left:
-            along, received = lax.optimization_barrier((along, received))
-        needed = lax.dynamic_slice_in_dim(along, row_id * deep, deep, 0)
-        if left:
-            child, needed = lax.optimization_barrier((child, needed))
-        gathered = lax.all_gather(needed, "col", axis=0, tiled=False)
-        gathered = gathered.reshape(-1, PANEL)
-
-        def factor_at(a, where):
-            group = a // 3
-            return ((group % col_count) * deep + group // col_count) * 3 + a % 3, 0
-    else:
+            received = more(received, left // BLK, 1)
+        span = strip_blocks * BLK
+        pieces = [jnp.where(row_id == part, strip, 0.0) for part in range(-(-PANEL // span))]
+        panel_t = lax.psum(jnp.concatenate(pieces, axis=0)[:PANEL], "row")
+        cols_factor = column_factor(panel_t, pivot_inverse)
         gathered = lax.all_gather(cols_factor, ("sub", "col"), axis=0, tiled=False)
         gathered = lax.dynamic_slice_in_dim(gathered, row_id * group_rows, group_rows, 0)
-        gathered = gathered.reshape(-1, PANEL)
-
-        def factor_at(a, where):
-            return a, 0
-
-    if left:
-        received = exchange(child, received, head + half, left - half, 3, count, 2)
+        first = second = gathered.reshape(-1, PANEL)
+
+        def factor_at(a):
+            return a
+
+        second_at = 1
+
     return pl.pallas_call(
         functools.partial(final_kernel, count, panel_blocks),
         grid_spec=pltpu.PrefetchScalarGridSpec(
@@ -295,11 +321,15 @@
             in_specs=[smem, front_spec]
             + piece_specs(count, 2)
             + [
-                pl.BlockSpec((BLK, PANEL), factor_at),
+                pl.BlockSpec((BLK, PANEL // 2), lambda a, where: (factor_at(a), 0)),
+                pl.BlockSpec((BLK, PANEL // 2), lambda a, where: (factor_at(a), second_at)),
                 pl.BlockSpec((group_cols, PANEL), lambda a, where: (0, 0)),
             ],
             out_specs=front_spec,
-            scratch_shapes=[pltpu.VMEM((group_cols, PANEL), jnp.bfloat16)] * 2,
+            scratch_shapes=[
+                pltpu.VMEM((group_cols, 3 * PANEL), jnp.bfloat16),
+                pltpu.VMEM((BLK, PANEL), jnp.float32),
+            ],
         ),
         out_shape=jax.ShapeDtypeStruct((row_blocks * BLK, group_cols), jnp.float32),
         compiler_params=pltpu.CompilerParams(vmem_limit_bytes=48 * 2**20),
@@ -308,7 +338,7 @@
             bytes_accessed=100 * 2**20,
             transcendentals=0,
         ),
-    )(where, weights, front_in, *([received] * count), gathered, cols_factor)
+    )(where, weights, front_in, *([received] * count), first, second, cols_factor)
 
 
 def solution(mesh):

time: 1220 us -> 1050 us (0.86)
  Pallas kernels: 1090 us -> 988 us
  waiting for transfers between devices: 70.9 us -> 0.12 us
    pallas_call x3 -> x5, Pallas kernels: 1010 us -> 909 us  [exchange(): pl.pallas_call(functools.partial(exchange_kernel, count, first, rows, chu...]
    ppermute x1, waiting for transfers between devices: 70.9 us -> 0.01 us  [shards(): other = lax.ppermute(strip, 'row', [(0, 1)])]
  transfers between devices with their start and end apart: 3 -> 5, of which waited for: 1 -> 0; matrix products, arithmetic and copies ran while one was open for 0% -> 0% of each run, Pallas kernels for 65% -> 67%
where the time goes in v2:
time: 1050 us; the launch traced here: 1040 us
  Pallas kernels  988 us (94%)
  blocking collectives  15.8 us (2%)
  between operations  13.3 us (1%)
  matrix products  12.9 us (1%)
  local copies, waits for them, and re-layouts  11.1 us (1%)
    pallas_call x5, Pallas kernels, exchange(): pl.pallas_call(functools.partial(exchange_kernel, count, first, rows, chu...  909 us
    pallas_call x1, Pallas kernels, shards(): pl.pallas_call(functools.partial(final_kernel, count, panel_blocks), grid...  71.5 us
  transfers between devices with their start and end apart: 5, of which 0 were waited for; matrix products, arithmetic and copies ran while one was open for 0% of the time, Pallas kernels for 67%

profile of v2, /device:TPU:15, one launch (start us, length us, event | category | flops | bytes accessed | tf_op | source)
XLA Modules:
  0.0 1045.0 jit_solution(5625042018567790279)
XLA Ops:
  6.5 0.0 copy-start
  6.5 0.0 all-gather.7.cloned.1.call-start
  6.5 0.7 copy-done
  7.2 0.1 constant_dynamic-slice_fusion.5
  7.3 0.1 broadcast_compare_fusion
  7.4 0.1 select_reduce_fusion.1
  7.5 0.7 convert_element_type.5
  8.2 15.8 %all_gather.22 = f32[16,16,8]{1,2,0:T(8,128)S(1)} all-gather(f32[1,16,8]{1,2,0:T(8,128)S(1)} %convert_element_type.5), channel_id=1, replica_groups=mesh['sub'=4,'row'=2,'col'=4] {'sub','col'}, dimensions={0}, use_global_device_ids=true | all-gather | bytes 8704 | tf_op jit(solution)/shard_map/all_gather | solution.py:216
  24.0 0.1 constant_dynamic-slice_fusion.4
  24.0 0.1 select_reduce_fusion
  24.2 0.1 copy.14
  24.3 0.1 broadcast_compare_fusion.1
  24.4 0.7 select_n.69.weights
  25.1 0.1 copy.13
  25.2 0.1 select_n.65
  25.3 203.8 %shard_map.55 = (f32[4,1024,512]{2,1,0:T(8,128)}, f32[4,4096,512]{2,1,0:T(8,128)}) custom-call(f32[1,4096,2048]{2,1,0:T(8,128)} %refs_0_.5), custom_call_target="tpu_custom_call" | custom-call | bytes 671088640 | tf_op jit(solution)/shard_map/pallas_call | solution.py:108
  229.2 0.7 pad_add_fusion.where
  229.8 7.5 shard_map.56
  237.3 1.3 collective-permute-start
  238.6 106.1 %shard_map.57 = (f32[4,512,512]{2,1,0:T(8,128)}, f32[4,4096,512]{2,1,0:T(8,128)}) custom-call(f32[1,4096,2048]{2,1,0:T(8,128)} %refs_0_.5, f32[4,4096,512]{2,1,0:T(8,128)} %get-tuple-element.25.refs_0_.refs_1_.refs_2_.refs_3_), custom_call_target="tpu_custom_call", output_to_operand_aliasing={{1}: (1, {})} | custom-call | bytes 335544320 | tf_op jit(solution)/shard_map/pallas_call | solution.py:108
  344.7 0.0 collective-permute-done
  344.7 0.0 copy-start.4
  344.7 1.6 copy-done.4
  346.4 12.9 %fusion.refs_6_ = f32[768,1024]{1,0:T(8,128)S(1)} fusion(f32[1024,1024]{1,0:T(8,128)} %param.9, f32[1024,768]{1,0:T(8,128)} %shard_map.56, f32[1024,768]{1,0:T(8,128)} %copy-done.4, pred[]{:T(512)S(6)} %eq.44), kind=kOutput, calls=%fused_computation | convolution fusion | flops 4832624640 | bytes 13631489 | tf_op jit(solution)/shard_map/dot_general | solution.py:188
  359.3 1.3 constant_dynamic-slice_fusion.2
  360.6 0.0 all-gather.7.cloned.1.call-update
  360.6 0.0 all-gather.9.cloned.1.call-start
  360.7 250.5 %shard_map.58 = (f32[4,768,512]{2,1,0:T(8,128)}, f32[4,4096,512]{2,1,0:T(8,128)}) custom-call(f32[1,4096,2048]{2,1,0:T(8,128)} %refs_0_.5, f32[4,4096,512]{2,1,0:T(8,128)} %get-tuple-element.32.refs_1_), custom_call_target="tpu_custom_call", output_to_operand_aliasing={{1}: (1, {})} | custom-call | bytes 503316480 | tf_op jit(solution)/shard_map/pallas_call | solution.py:108
  611.2 0.0 all-gather.7.cloned.1.call-done
  611.2 6.3 constant_dynamic-slice_fusion
  617.5 0.0 all-gather.9.cloned.1.call-update
  617.6 0.2 all-gather.11.cloned.1.call-start
  617.8 0.3 collective-permute-start.1
  618.1 152.8 %shard_map.59 = (f32[4,768,512]{2,1,0:T(8,128)}, f32[4,4096,512]{2,1,0:T(8,128)}) custom-call(f32[1,4096,2048]{2,1,0:T(8,128)} %refs_0_.5, f32[4,4096,512]{2,1,0:T(8,128)} %get-tuple-element.37.refs_1_), custom_call_target="tpu_custom_call", output_to_operand_aliasing={{1}: (1, {})} | custom-call | bytes 503316480 | tf_op jit(solution)/shard_map/pallas_call | solution.py:108
  771.0 0.0 collective-permute-done.1
  771.0 0.0 all-gather.11.cloned.1.call-update
  771.0 0.0 copy-start.2
  771.0 0.0 copy-start.3
  771.0 195.8 %shard_map.60 = (f32[4,1024,512]{2,1,0:T(8,128)}, f32[4,4096,512]{2,1,0:T(8,128)}) custom-call(f32[1,4096,2048]{2,1,0:T(8,128)} %refs_0_.5, f32[4,4096,512]{2,1,0:T(8,128)} %get-tuple-element.41.refs_1_), custom_call_target="tpu_custom_call", output_to_operand_aliasing={{1}: (1, {})} | custom-call | bytes 671088640 | tf_op jit(solution)/shard_map/pallas_call | solution.py:108
  966.8 0.0 all-gather.9.cloned.1.call-done
  966.9 0.0 all-gather.11.cloned.1.call-done
  966.9 0.0 copy-done.2
  966.9 0.0 copy-done.3
  966.9 0.0 copy-start.1
  966.9 71.5 %shard_map.61 = f32[6144,768]{1,0:T(8,128)} custom-call(s32[98]{0:T(128)S(1)} %copy-done.3, f32[576]{0:T(1024)S(1)} %copy-done.2, f32[6144,768]{1,0:T(8,128)} %front.3, f32[4,4096,512]{2,1,0:T(8,128)} %get-tuple-element.42.refs_0_.refs_1_.refs_2_.refs_3_, f32[4,4096,512]{2,1,0:T(8,128)} %get-tuple-element.42.refs_0_.refs_1_.refs_2_.refs_3_, ...), custom_call_target="tpu_custom_call" | custom-call | flops 28991029248 | bytes 104857600 | tf_op jit(solution)/shard_map/pallas_call | solution.py:316
  1038.4 0.0 copy-done.1
  (6 shorter events, 0.1 us)
Async XLA Ops:
  6.5 0.7 copy-start
  6.5 604.7 %all-gather.7.cloned.1.call-start = ((), (), s32[]{:S(2)}) async-start(), calls=%async_computation | async-start | bytes 7864320 | tf_op jit(solution)/shard_map/all_gather | solution.py:277
  237.3 107.5 %collective-permute-start = (f32[1024,768]{1,0:T(8,128)}, f32[1024,768]{1,0:T(8,128)S(1)}, u32[]{:S(2)}, u32[]{:S(2)}) collective-permute-start(f32[1024,768]{1,0:T(8,128)} %shard_map.56), channel_id=1, source_target_pairs={{0,4},{1,5},{2,6},{3,7},{8,12},{9,13},{10,14},{11,15},{16,20},{17,... | collective-permute-start | bytes 9437192 | tf_op jit(solution)/shard_map/ppermute | solution.py:266
  344.7 1.6 copy-start.4
  360.6 606.2 %all-gather.9.cloned.1.call-start = ((), (), s32[]{:S(2)}) async-start(), calls=%async_computation.1 | async-start | bytes 15728640 | tf_op jit(solution)/shard_map/all_gather | solution.py:286
  617.6 349.3 %all-gather.11.cloned.1.call-start = ((), (), s32[]{:S(2)}) async-start(), calls=%async_computation.2 | async-start | bytes 15728640 | tf_op jit(solution)/shard_map/all_gather | solution.py:292
  617.8 153.2 %collective-permute-start.1 = (f32[2,768,512]{2,1,0:T(8,128)}, f32[2,768,512]{2,1,0:T(8,128)}, u32[]{:S(2)}, u32[]{:S(2)}) collective-permute-start(f32[2,768,512]{2,1,0:T(8,128)} %get-tuple-element.36), channel_id=1, source_target_pairs={{0,4},{4,0},{1,5},{5,1},{2,6},{6,2},{3,7},{7,3},{8,12},{12,8},{9,1... | collective-permute-start | bytes 9437192 | tf_op jit(solution)/shard_map/ppermute | solution.py:285
  771.0 195.9 %copy-start.2 = (f32[576]{0:T(1024)S(1)}, f32[576]{0:T(1024)}, u32[]{:S(2)}) copy-start(f32[576]{0:T(1024)} %select_n.69.weights) | copy-start | bytes 6916
  771.0 195.9 %copy-start.3 = (s32[98]{0:T(128)S(1)}, s32[98]{0:T(128)}, u32[]{:S(2)}) copy-start(s32[98]{0:T(128)} %pad_add_fusion.where) | copy-start | bytes 1180
  966.9 71.5 %copy-start.1 = (s32[4,32]{1,0:T(4,128)S(1)}, s32[4,32]{1,0:T(4,128)}, u32[]{:S(2)}) copy-start(s32[4,32]{1,0:T(4,128)} %param.8) | copy-start | bytes 1540
Sparse Core Ops, SparseCore 0:
  360.8 227.7 all-gather.6
  617.7 140.2 all-gather.8
  771.1 151.9 all-gather.10

commit v3 on v2

--- a/solution.py
+++ b/solution.py
@@ -143,14 +143,13 @@
 def final_kernel(count, panel_blocks, where, weights, front, *refs):
     pieces = refs[:count]
     rows_first, rows_second, cols_factor, out, right, rows_factor = refs[count:]
-    a = pl.program_id(0)
-    row_block = where[0] + a
+    group = pl.program_id(0)
 
     def split(value):
         top = value.astype(jnp.bfloat16)
         return top, (value - top.astype(jnp.float32)).astype(jnp.bfloat16)
 
-    @pl.when(a == 0)
+    @pl.when(group == 0)
     def _():
         top, rest = split(cols_factor[...])
         right[:, :PANEL] = rest
@@ -164,17 +163,27 @@
     for column in range(3):
         col_block = where[1] + column
         span = slice(column * BLK, (column + 1) * BLK)
-        here = extended_columns(weights, a, front, pieces, column)
         update = lax.dot_general(
             left, right[span, :], (((1,), (1,)), ((), ())), preferred_element_type=jnp.float32
         )
-        both = jnp.logical_and(row_block >= panel_blocks, col_block >= panel_blocks)
-        out[:, span] = jnp.where(both, here - update, here)
-
-        @pl.when(jnp.logical_and(row_block >= panel_blocks, col_block < panel_blocks))
-        def _():
-            source = jnp.minimum(col_block, panel_blocks - 1) * BLK
-            out[:, span] = rows_factor[:, pl.ds(pl.multiple_of(source, BLK), BLK)]
+        for place in range(3):
+            a = group * 3 + place
+            row_block = where[0] + a
+            band = slice(place * BLK, (place + 1) * BLK)
+            here = front[band, span]
+            for s, piece in enumerate(pieces):
+                at = (where[2 + a * count + s] - 2 * group) * BLK
+                held = pl.ds(pl.multiple_of(at, BLK), BLK)
+                for j in range(2):
+                    weight = weights[((a * count + s) * 3 + column) * 2 + j]
+                    here = here + weight * piece[0, held, j * BLK : (j + 1) * BLK]
+            both = jnp.logical_and(row_block >= panel_blocks, col_block >= panel_blocks)
+            out[band, span] = jnp.where(both, here - update[band, :], here)
+
+            @pl.when(jnp.logical_and(row_block >= panel_blocks, col_block < panel_blocks))
+            def _():
+                source = jnp.minimum(col_block, panel_blocks - 1) * BLK
+                out[band, span] = rows_factor[band, pl.ds(pl.multiple_of(source, BLK), BLK)]
 
 
 def piece_specs(count, offset):
@@ -237,7 +246,7 @@
 
     rows = child_rows * BLK
     head = min(rows, 4 * BLK)
-    received = exchange(child_updates, None, 0, head, head // BLK, count, 0)
+    received = exchange(child_updates, None, 0, head, 2 * head // BLK, count, 0)
     strip_blocks = min(panel_blocks, row_blocks)
     smem = pl.BlockSpec(memory_space=pltpu.SMEM)
     front_spec = pl.BlockSpec((BLK, group_cols), lambda a, where: (a, 0))
@@ -258,7 +267,7 @@
     done = head
 
     def more(received, blocks, ident):
-        return exchange(child, received, done, blocks * BLK, blocks, count, ident)
+        return exchange(child, received, done, blocks * BLK, 2 * blocks, count, ident)
 
     if row_count == 2 and strip_blocks == panel_blocks:
         parts = (2, 3, 3, left // BLK - 8)
@@ -292,9 +301,8 @@
         second = lax.all_gather(second, "col", axis=0, tiled=False).reshape(-1, wide)
         received = more(received, parts[3], 4)
 
-        def factor_at(a):
-            group = a // 3
-            return ((group % col_count) * deep + group // col_count) * 3 + a % 3
+        def factor_at(group):
+            return (group % col_count) * deep + group // col_count
 
         second_at = 0
     else:
@@ -308,31 +316,34 @@
         gathered = lax.dynamic_slice_in_dim(gathered, row_id * group_rows, group_rows, 0)
         first = second = gathered.reshape(-1, PANEL)
 
-        def factor_at(a):
-            return a
+        def factor_at(group):
+            return group
 
         second_at = 1
 
+    group_spec = pl.BlockSpec((group_cols, group_cols), lambda a, where: (a, 0))
+    group_pieces = [
+        pl.BlockSpec((1, 2 * BLK, 2 * BLK), lambda a, where, s=s: (s, a, 0)) for s in range(count)
+    ]
     return pl.pallas_call(
         functools.partial(final_kernel, count, panel_blocks),
         grid_spec=pltpu.PrefetchScalarGridSpec(
             num_scalar_prefetch=1,
-            grid=(row_blocks,),
-            in_specs=[smem, front_spec]
-            + piece_specs(count, 2)
+            grid=(row_blocks // 3,),
+            in_specs=[smem, group_spec] + group_pieces
             + [
-                pl.BlockSpec((BLK, PANEL // 2), lambda a, where: (factor_at(a), 0)),
-                pl.BlockSpec((BLK, PANEL // 2), lambda a, where: (factor_at(a), second_at)),
+                pl.BlockSpec((group_cols, PANEL // 2), lambda a, where: (factor_at(a), 0)),
+                pl.BlockSpec((group_cols, PANEL // 2), lambda a, where: (factor_at(a), second_at)),
                 pl.BlockSpec((group_cols, PANEL), lambda a, where: (0, 0)),
             ],
-            out_specs=front_spec,
+            out_specs=group_spec,
             scratch_shapes=[
                 pltpu.VMEM((group_cols, 3 * PANEL), jnp.bfloat16),
-                pltpu.VMEM((BLK, PANEL), jnp.float32),
+                pltpu.VMEM((group_cols, PANEL), jnp.float32),
             ],
         ),
         out_shape=jax.ShapeDtypeStruct((row_blocks * BLK, group_cols), jnp.float32),
-        compiler_params=pltpu.CompilerParams(vmem_limit_bytes=48 * 2**20),
+        compiler_params=pltpu.CompilerParams(vmem_limit_bytes=58 * 2**20),
         cost_estimate=pl.CostEstimate(
             flops=6 * row_blocks * BLK * group_cols * PANEL,
             bytes_accessed=100 * 2**20,

time: 1050 us -> 1030 us (0.981)
  Pallas kernels: 988 us -> 967 us
    pallas_call x5, Pallas kernels: 909 us -> 887 us  [exchange(): pl.pallas_call(functools.partial(exchange_kernel, count, first, rows, chu...]
where the time goes in v3:
time: 1030 us
  Pallas kernels  967 us (94%)
  blocking collectives  15.8 us (2%)
  between operations  13.3 us (1%)
  local copies, waits for them, and re-layouts  12.9 us (1%)
  matrix products  12.9 us (1%)
    pallas_call x5, Pallas kernels, exchange(): pl.pallas_call(functools.partial(exchange_kernel, count, first, rows, chu...  887 us
    pallas_call x1, Pallas kernels, shards(): pl.pallas_call(functools.partial(final_kernel, count, panel_blocks), grid...  72.9 us
  transfers between devices with their start and end apart: 5, of which 0 were waited for; matrix products, arithmetic and copies ran while one was open for 0% of the time, Pallas kernels for 67%

profile of v3, /device:TPU:15, one launch (start us, length us, event | category | flops | bytes accessed | tf_op | source)
XLA Modules:
  0.0 1027.4 jit_solution(1024320775927087391)
XLA Ops:
  6.5 0.0 copy-start
  6.5 0.0 all-gather.7.cloned.1.call-start
  6.5 0.7 copy-done
  7.2 0.1 constant_dynamic-slice_fusion.5
  7.3 0.1 broadcast_compare_fusion
  7.4 0.1 select_reduce_fusion.1
  7.5 0.7 convert_element_type.5
  8.2 15.8 %all_gather.22 = f32[16,16,8]{1,2,0:T(8,128)S(1)} all-gather(f32[1,16,8]{1,2,0:T(8,128)S(1)} %convert_element_type.5), channel_id=1, replica_groups=mesh['sub'=4,'row'=2,'col'=4] {'sub','col'}, dimensions={0}, use_global_device_ids=true | all-gather | bytes 8704 | tf_op jit(solution)/shard_map/all_gather | solution.py:225
  24.0 0.1 constant_dynamic-slice_fusion.4
  24.0 0.1 select_reduce_fusion
  24.2 0.1 copy.14
  24.3 0.1 broadcast_compare_fusion.1
  24.4 0.7 select_n.69.weights
  25.1 0.1 copy.13
  25.2 0.1 select_n.65
  25.3 198.8 %shard_map.55 = (f32[4,1024,512]{2,1,0:T(8,128)}, f32[4,4096,512]{2,1,0:T(8,128)}) custom-call(f32[1,4096,2048]{2,1,0:T(8,128)} %refs_0_.5), custom_call_target="tpu_custom_call" | custom-call | bytes 671088640 | tf_op jit(solution)/shard_map/pallas_call | solution.py:108
  224.1 0.7 pad_add_fusion.where
  224.8 7.5 shard_map.56
  232.2 1.3 collective-permute-start
  233.5 101.1 %shard_map.57 = (f32[4,512,512]{2,1,0:T(8,128)}, f32[4,4096,512]{2,1,0:T(8,128)}) custom-call(f32[1,4096,2048]{2,1,0:T(8,128)} %refs_0_.5, f32[4,4096,512]{2,1,0:T(8,128)} %get-tuple-element.25.refs_0_.refs_1_.refs_2_.refs_3_), custom_call_target="tpu_custom_call", output_to_operand_aliasing={{1}: (1, {})} | custom-call | bytes 335544320 | tf_op jit(solution)/shard_map/pallas_call | solution.py:108
  334.7 0.0 collective-permute-done
  334.7 0.0 copy-start.4
  334.7 1.6 copy-done.4
  336.3 12.9 %fusion.refs_6_ = f32[768,1024]{1,0:T(8,128)S(1)} fusion(f32[1024,1024]{1,0:T(8,128)} %param.9, f32[1024,768]{1,0:T(8,128)} %shard_map.56, f32[1024,768]{1,0:T(8,128)} %copy-done.4, pred[]{:T(512)S(6)} %eq.44), kind=kOutput, calls=%fused_computation | convolution fusion | flops 4832624640 | bytes 13631489 | tf_op jit(solution)/shard_map/dot_general | solution.py:197
  349.2 0.0 copy-start.2
  349.2 1.5 constant_dynamic-slice_fusion.2
  350.7 0.0 all-gather.7.cloned.1.call-update
  350.7 0.0 all-gather.9.cloned.1.call-start
  350.8 246.4 %shard_map.58 = (f32[4,768,512]{2,1,0:T(8,128)}, f32[4,4096,512]{2,1,0:T(8,128)}) custom-call(f32[1,4096,2048]{2,1,0:T(8,128)} %refs_0_.5, f32[4,4096,512]{2,1,0:T(8,128)} %get-tuple-element.32.refs_1_), custom_call_target="tpu_custom_call", output_to_operand_aliasing={{1}: (1, {})} | custom-call | bytes 503316480 | tf_op jit(solution)/shard_map/pallas_call | solution.py:108
  597.2 0.0 copy-done.2
  597.2 0.0 all-gather.7.cloned.1.call-done
  597.2 6.3 constant_dynamic-slice_fusion
  603.5 0.0 all-gather.9.cloned.1.call-update
  603.5 0.2 all-gather.11.cloned.1.call-start
  603.8 2.2 collective-permute-start.1
  605.9 148.6 %shard_map.59 = (f32[4,768,512]{2,1,0:T(8,128)}, f32[4,4096,512]{2,1,0:T(8,128)}) custom-call(f32[1,4096,2048]{2,1,0:T(8,128)} %refs_0_.5, f32[4,4096,512]{2,1,0:T(8,128)} %get-tuple-element.37.refs_1_), custom_call_target="tpu_custom_call", output_to_operand_aliasing={{1}: (1, {})} | custom-call | bytes 503316480 | tf_op jit(solution)/shard_map/pallas_call | solution.py:108
  754.6 0.0 collective-permute-done.1
  754.6 0.0 copy-start.3
  754.6 1.7 copy-done.3
  756.2 0.0 all-gather.11.cloned.1.call-update
  756.3 191.7 %shard_map.60 = (f32[4,1024,512]{2,1,0:T(8,128)}, f32[4,4096,512]{2,1,0:T(8,128)}) custom-call(f32[1,4096,2048]{2,1,0:T(8,128)} %refs_0_.5, f32[4,4096,512]{2,1,0:T(8,128)} %get-tuple-element.41.refs_1_), custom_call_target="tpu_custom_call", output_to_operand_aliasing={{1}: (1, {})} | custom-call | bytes 671088640 | tf_op jit(solution)/shard_map/pallas_call | solution.py:108
  947.9 0.0 all-gather.9.cloned.1.call-done
  948.0 0.0 all-gather.11.cloned.1.call-done
  948.0 0.0 copy-start.1
  948.0 72.9 %shard_map.61 = f32[6144,768]{1,0:T(8,128)} custom-call(s32[98]{0:T(128)} %pad_add_fusion.where, f32[576]{0:T(1024)} %select_n.69.weights, f32[6144,768]{1,0:T(8,128)} %front.3, f32[4,4096,512]{2,1,0:T(8,128)} %get-tuple-element.42.refs_0_.refs_1_.refs_2_.refs_3_, f32[4,4096,512]{2,1,0:T(8,128)} %get-tuple-element.42.refs_0_.refs_1_.refs_2_.refs_3_, ...), custom_call_target="tpu_custom_call" | custom-call | flops 28991029248 | bytes 104857600 | tf_op jit(solution)/shard_map/pallas_call | solution.py:328
  1020.9 0.0 copy-done.1
  (6 shorter events, 0.1 us)
Async XLA Ops:
  6.5 0.7 copy-start
  6.5 590.6 %all-gather.7.cloned.1.call-start = ((), (), s32[]{:S(2)}) async-start(), calls=%async_computation | async-start | bytes 7864320 | tf_op jit(solution)/shard_map/all_gather | solution.py:286
  232.2 102.5 %collective-permute-start = (f32[1024,768]{1,0:T(8,128)}, f32[1024,768]{1,0:T(8,128)S(1)}, u32[]{:S(2)}, u32[]{:S(2)}) collective-permute-start(f32[1024,768]{1,0:T(8,128)} %shard_map.56), channel_id=1, source_target_pairs={{0,4},{1,5},{2,6},{3,7},{8,12},{9,13},{10,14},{11,15},{16,20},{17,... | collective-permute-start | bytes 9437192 | tf_op jit(solution)/shard_map/ppermute | solution.py:275
  334.7 1.6 copy-start.4
  349.2 247.9 %copy-start.2 = (f32[768,1024]{1,0:T(8,128)}, f32[768,1024]{1,0:T(8,128)S(1)}, u32[]{:S(2)}) copy-start(f32[768,1024]{1,0:T(8,128)S(1)} %fusion.refs_6_) | copy-start | bytes 9437188
  350.7 597.2 %all-gather.9.cloned.1.call-start = ((), (), s32[]{:S(2)}) async-start(), calls=%async_computation.1 | async-start | bytes 15728640 | tf_op jit(solution)/shard_map/all_gather | solution.py:295
  603.5 344.5 %all-gather.11.cloned.1.call-start = ((), (), s32[]{:S(2)}) async-start(), calls=%async_computation.2 | async-start | bytes 15728640 | tf_op jit(solution)/shard_map/all_gather | solution.py:301
  603.8 150.8 %collective-permute-start.1 = (f32[2,768,512]{2,1,0:T(8,128)}, f32[2,768,512]{2,1,0:T(8,128)S(1)}, u32[]{:S(2)}, u32[]{:S(2)}) collective-permute-start(f32[2,768,512]{2,1,0:T(8,128)} %get-tuple-element.36), channel_id=1, source_target_pairs={{0,4},{4,0},{1,5},{5,1},{2,6},{6,2},{3,7},{7,3},{8,12},{12,8},{9,1... | collective-permute-start | bytes 9437192 | tf_op jit(solution)/shard_map/ppermute | solution.py:294
  754.6 1.7 copy-start.3
  948.0 72.9 %copy-start.1 = (s32[4,32]{1,0:T(4,128)S(1)}, s32[4,32]{1,0:T(4,128)}, u32[]{:S(2)}) copy-start(s32[4,32]{1,0:T(4,128)} %param.8) | copy-start | bytes 1540
Sparse Core Ops, SparseCore 0:
  350.9 230.2 all-gather.6
  603.6 143.6 all-gather.8
  756.4 147.6 all-gather.10
